TPU v7x, 256 devices: a whole 4x4x8 slice. The times are simulated.
256 devices in a mesh: row: 64 (over z, y, x_hi), col: 2 (over core), layer: 2 (over x_lo).
Axes of the slice: x: 4 (x_hi: 2, x_lo: 2; x = x_hi * 2 + x_lo), y: 4, z: 8, core: 2. Of those that a mesh axis runs over, the one named last changes fastest.
Arguments:
- a_blocks: bfloat16 [64, 128, 64, 64], P('row', ('col', 'layer')), may hold values from -6 to 6
- a_index: int32 [64, 128, 2], P('row', ('col', 'layer')), may hold values from 0 to 511, as said below
- a_count: int32 [64, 4], P('row', ('col', 'layer')), may hold values from 1 to 32, as said below
- b_blocks: bfloat16 [512, 2, 64, 64], P(('row', 'layer'), 'col'), may hold values from -0.75 to 0.75
- b_index: int32 [512, 2, 2], P(('row', 'layer'), 'col'), may hold values from 0 to 15, as said below
- b_count: int32 [128, 2], P(('row', 'layer'), 'col'), may hold values from 1 to 4, as said below
Outputs:
- product: bfloat16 [32768, 1024], P(('row', 'layer'), 'col')
Inputs may be any that keep to these rules, and one draw needn't show every extreme that they name: `a_index`: within one piece the live slots name distinct (block row, inner block) positions; entry 0 is below 8, entry 1 below 512. `b_index`: within one piece the live slots name distinct (inner block, block column) positions; entry 0 is below 16, entry 1 below 8. `a_count`: some piece is full. `b_count`: some piece is full.
All inputs are finite; a program needn't handle non-finite values.
Results may differ from a plain program's by a relative error of at most 0.001.
Values may be sent and summed in bfloat16 or wider, within the bound.
No kernel may reach another device: no remote copies, remote signals or barrier semaphores. Data moves between devices by JAX's collectives and lax.ppermute only.
A program may use at most 128 MiB of HBM per device.

v0:
```python
import math

import jax
import jax.numpy as jnp
from jax import lax
from jax.sharding import PartitionSpec as P

BLK = 64
NB = 2048
RW = 8
KW = 8


def tile_product(a_vals, a_rows, a_keys, b_vals, b_keys, b_cols, row_count, col_count):
    count = b_vals.shape[0]
    hit = (a_keys[:, None, None] == b_keys[None, None, :]) & (
        b_cols[None, None, :] == jnp.arange(col_count, dtype=jnp.int32)[None, :, None]
    )
    chosen = jnp.sum(jnp.where(hit, jnp.arange(count, dtype=jnp.int32)[None, None, :], 0), axis=2)
    found = jnp.any(hit, axis=2)
    picked = b_vals[chosen] * found[:, :, None, None].astype(b_vals.dtype)
    terms = jnp.einsum("axy,ajyz->axjz", a_vals, picked, preferred_element_type=jnp.float32)
    place = (a_rows[:, None] == jnp.arange(row_count, dtype=jnp.int32)[None, :]).astype(jnp.float32)
    summed = jnp.dot(place.T, terms.reshape(terms.shape[0], -1), precision=lax.Precision.HIGHEST)
    return summed.reshape(row_count * BLK, col_count * BLK)


def on_device(a_blocks, a_index, a_count, b_blocks, b_index, b_count):
    slots_a = a_blocks.shape[1]
    slots_b = b_blocks.shape[0]
    layers = lax.axis_size("layer")
    inner_a = NB // (layers * lax.axis_size("col"))
    inner_b = NB // (layers * lax.axis_size("row"))
    a_keys = jnp.where(jnp.arange(slots_a, dtype=jnp.int32) < a_count[0, 0], a_index[0, :, 1], -1)[
        None, :
    ]
    a_rows = a_index[0, :, 0][None, :]
    b_keys = jnp.where(jnp.arange(slots_b, dtype=jnp.int32) < b_count[0, 0], b_index[:, 0, 0], -1)[
        :, None
    ]
    b_cols = b_index[:, 0, 1][:, None]
    b_vals, b_raw, b_col_all = (
        lax.all_gather(b_blocks, "row", axis=0, tiled=True),
        lax.all_gather(b_keys, "row", axis=0, tiled=True),
        lax.all_gather(b_cols, "row", axis=0, tiled=True),
    )
    piece_b = jnp.arange(b_raw.shape[0], dtype=jnp.int32) // slots_b
    b_glob = jnp.where(b_raw[:, 0] >= 0, piece_b * inner_b + b_raw[:, 0], -2).astype(jnp.int32)
    row_count = RW
    b_flat = b_vals[:, 0]
    b_col_flat = b_col_all[:, 0]
    empty = jnp.zeros((row_count * BLK, KW * BLK), jnp.float32)

    def fold_rows(total, vals, rows, glob):
        taken = glob.shape[0]
        step = slots_a * math.gcd(taken // slots_a, 8)
        turns = taken // step

        def one_turn(index, acc):
            return acc + tile_product(vals, rows, glob, b_flat, b_glob, b_col_flat, row_count, KW)

        return lax.fori_loop(0, turns, one_turn, total)

    vals = lax.all_gather(a_blocks, "col", axis=1, tiled=True)
    keys = lax.all_gather(a_keys, "col", axis=1, tiled=True)
    rows = lax.all_gather(a_rows, "col", axis=1, tiled=True)
    taken = keys.shape[1]
    group = jnp.arange(taken, dtype=jnp.int32) // slots_a
    glob = jnp.where(keys[0] >= 0, group * inner_a + keys[0], -1).astype(jnp.int32)
    partial_tile = fold_rows(empty, vals[0], rows[0], glob)
    return lax.psum_scatter(partial_tile, "layer", scatter_dimension=0, tiled=True).astype(
        jnp.bfloat16
    )


def solution(mesh):
    in_specs = (
        P("row", ("col", "layer"), None, None),
        P("row", ("col", "layer"), None),
        P("row", ("col", "layer")),
        P(("row", "layer"), "col", None, None),
        P(("row", "layer"), "col", None),
        P(("row", "layer"), "col"),
    )
    out_specs = P(("row", "layer"), "col")
    return jax.shard_map(
        on_device, mesh=mesh, in_specs=in_specs, out_specs=out_specs, check_vma=False
    )
```

profile of v0, /device:TPU:2, one launch (start us, length us, event | category | flops | bytes accessed | tf_op | source)
XLA Modules:
  0.0 253.7 jit_solution(8151125068441532517)
XLA Ops:
  6.5 0.0 all-gather.4.cloned.1.call-start
  6.5 0.7 all-gather.4.cloned.1.call-update
  7.3 0.0 reduce-scatter.2.cloned.1.call-start
  8.6 1.3 dynamic-slice.2
  9.9 1.3 dynamic-slice
  12.4 0.8 bitcast_dynamic-update-slice_fusion.1
  13.2 0.8 fusion.11
  14.0 1.8 all-reduce.5
  15.8 0.8 bitcast_dynamic-update-slice_fusion
  16.6 0.8 fusion.13
  17.3 27.9 %all-reduce.4 = (s32[256]{0:T(256)S(1)}, s32[256]{0:T(256)S(1)}) all-reduce(s32[256]{0:T(256)S(1)} %bitcast_dynamic-update-slice_fusion, s32[256]{0:T(256)S(1)} %fusion.13), channel_id=3, replica_groups=mesh['row'=64,'col'=2,'layer'=2] {'row'}, use_global_device_ids=true, to_apply=%add.3 | all-reduce | flops 512 | bytes 4096
  45.3 0.1 broadcast_compare_fusion
  45.4 1.2 and_reduce_fusion
  46.6 1.2 fusion.3
  47.8 0.1 reshape.170
  47.9 2.8 %all_gather.23 = bf16[1,64,64,64]{3,2,0,1:T(8,128)(2,1)S(1)} all-gather(bf16[1,32,64,64]{3,2,0,1:T(8,128)(2,1)} %bitcast.42), channel_id=1, replica_groups=mesh['row'=64,'col'=2,'layer'=2] {'col'}, dimensions={1}, use_global_device_ids=true | all-gather | bytes 786432 | tf_op jit(solution)/shard_map/all_gather | solution.py:64
  50.6 90.8 %all-gather.4.cloned.1.call-done = bf16[256,1,64,64]{3,2,1,0:T(8,128)(2,1)} async-done(((bf16[4,1,64,64]{3,2,1,0:T(8,128)(2,1)}), bf16[256,1,64,64]{3,2,1,0:T(8,128)(2,1)}) %all-gather.4.cloned.1.call-update) | async-done | bytes 2097168 | tf_op jit(solution)/shard_map/all_gather | solution.py:43
  141.5 21.7 %gather_fusion = bf16[512,64,64]{2,1,0:T(8,128)(2,1)} fusion(bf16[256,64,64]{2,1,0:T(8,128)(2,1)} %bitcast.41, s32[1024]{0:T(1024)S(1)} %pad_clamp_fusion), kind=kCustom, calls=%fused_computation | custom fusion | bytes 8390656 | tf_op jit(solution)/shard_map/while/body/eval_jaxpr/gather | solution.py:21
  163.2 11.9 %copy.13 = bf16[64,8,64,64]{2,3,1,0:T(8,128)(2,1)} copy(bf16[64,8,64,64]{3,2,1,0:T(8,128)(2,1)} %bitcast.40) | data formatting | bytes 8388608 | tf_op jit(solution)/shard_map/while/body/eval_jaxpr/gather | solution.py:21
  175.2 11.5 %convolution_bitcast_fusion = f32[64,64,8,64]{1,3,2,0:T(8,128)} fusion(bf16[64,8,64,64]{2,3,1,0:T(8,128)(2,1)} %copy.13, bf16[64,8]{1,0:T(8,128)(2,1)S(1)} %convert_element_type.14, bf16[1,64,64,64]{3,2,0,1:T(8,128)(2,1)S(1)} %all_gather.23), kind=kOutput, calls=%fused_computation.1 | convolution fusion | flops 270532608 | bytes 13108224 | tf_op jit(solution)/shard_map/while/body/eval_jaxpr/axy,ajyz->axjz/dot_general | solution.py:22
  186.6 17.5 %copy.15 = f32[64,64,8,64]{3,2,1,0:T(8,128)} copy(f32[64,64,8,64]{1,3,2,0:T(8,128)} %convolution_bitcast_fusion) | data formatting | bytes 16777216 | tf_op jit(solution)/shard_map/while/body/eval_jaxpr/axy,ajyz->axjz/dot_general | solution.py:22
  204.1 12.9 %reshape.166 = f32[64,32768]{1,0:T(8,128)} reshape(f32[64,64,8,64]{3,2,1,0:T(8,128)} %copy.15) | data formatting | bytes 16777216 | tf_op jit(solution)/shard_map/while/body/eval_jaxpr/reshape | solution.py:24
  217.0 5.2 %fusion.4 = f32[8,32768]{1,0:T(8,128)S(1)} fusion(f32[64,32768]{1,0:T(8,128)} %reshape.166, s32[64]{0:T(128)S(1)} %get-tuple-element.22), kind=kOutput, calls=%fused_computation.11 | convolution fusion | flops 201327104 | bytes 9437440 | tf_op jit(solution)/shard_map/while/body/eval_jaxpr/dot_general | solution.py:24
  222.2 1.2 reshape.167
  223.3 0.0 reduce-scatter.2.cloned.1.call-update
  223.4 21.7 %reduce-scatter.2.cloned.1.call-done = f32[256,512]{1,0:T(8,128)} async-done(((f32[512,512]{1,0:T(8,128)}), f32[256,512]{1,0:T(8,128)}) %reduce-scatter.2.cloned.1.call-update) | async-done | bytes 524304 | tf_op jit(solution)/shard_map/reduce_scatter | solution.py:71
  245.1 1.8 convert_element_type.15
  (10 shorter events, 0.1 us)
Async XLA Ops:
  6.5 134.9 %all-gather.4.cloned.1.call-start = ((), (), s32[]{:S(2)}) async-start(), calls=%async_computation.1 | async-start | bytes 4259840 | tf_op jit(solution)/shard_map/all_gather | solution.py:43
  7.3 237.8 %reduce-scatter.2.cloned.1.call-start = ((), (), s32[]{:S(2)}) async-start(), calls=%async_computation.2 | async-start | bytes 1572864 | tf_op jit(solution)/shard_map/reduce_scatter | solution.py:71
Sparse Core Ops, SparseCore 0:
  11.1 130.3 all-gather.3
  223.5 21.5 reduce-scatter.1
where the time goes:
time: 257 us; the launch traced here: 254 us
  waiting for transfers between devices  113 us (44%)
  local copies, waits for them, and re-layouts  69.4 us (27%)
  blocking collectives  32.5 us (13%)
  matrix products  16.7 us (6%)
  between operations  16 us (6%)
  other arithmetic  5.76 us (2%)
    all_gather x1, waiting for transfers between devices, on_device(): lax.all_gather(b_blocks, 'row', axis=0, tiled=True)  90.8 us
    gather x2, local copies, waits for them, and re-layouts, tile_product(): picked = b_vals[chosen] * found[:, :, None, None].astype(b_vals.dtype)  33.7 us
    unnamed x1, blocking collectives  27.9 us
    reduce_scatter x1, waiting for transfers between devices, on_device(): lax.psum_scatter(partial_tile, 'layer', scatter_dimension=0, tiled=True)  21.7 us
    dot_general x1, local copies, waits for them, and re-layouts, tile_product(): jnp.einsum('axy,ajyz->axjz', a_vals, picked, preferred_element_type=jnp.f...  17.5 us
    reshape x1, local copies, waits for them, and re-layouts, tile_product(): terms.reshape(terms.shape[0], -1)  12.9 us
    dot_general x1, matrix products, tile_product(): jnp.einsum('axy,ajyz->axjz', a_vals, picked, preferred_element_type=jnp.f...  11.5 us
    dot_general x1, matrix products, tile_product(): jnp.dot(place.T, terms.reshape(terms.shape[0], -1), precision=lax.Precisi...  5.18 us
  transfers between devices with their start and end apart: 2, of which 2 were waited for; matrix products, arithmetic and copies ran while one was open for 3% of the time, Pallas kernels for 0%

commit v1 on v0

v1 whole, which is shorter than its diff:
```python
import functools

import jax
import jax.numpy as jnp
from jax import lax
from jax.experimental import pallas as pl
from jax.experimental.pallas import tpu as pltpu
from jax.sharding import PartitionSpec as P

BLK = 64
SLOTS_A = 32
SLOTS_B = 4
INNER_A = 512
INNER_B = 16
RW = 8
KW = 8
LANES = 128
TAIL = 16
RING = 8
PLANE = 8
PIECE_ROWS = SLOTS_B * BLK * BLK // LANES
STAGE_ROWS = RING * PIECE_ROWS + TAIL
HALF_ROWS = RW * BLK // 2
COLS = KW * BLK
DEAD = 255.0

Z_GROUPS = [[z * PLANE + q for z in range(RING)] for q in range(PLANE)]
PLANE_GROUPS = [[z * PLANE + q for q in range(PLANE)] for z in range(RING)]

VMEM = pl.BlockSpec(memory_space=pltpu.VMEM)
SMEM = pl.BlockSpec(memory_space=pltpu.SMEM)
ANY = pl.BlockSpec(memory_space=pl.ANY)


def pack_kernel(b_ref, index_ref, count_ref, out_ref, piece):
    z = lax.axis_index("row") // PLANE
    blocks = [b_ref[s, 0].astype(jnp.float32) for s in range(SLOTS_B)]
    for pair in range(SLOTS_B // 2):
        both = jnp.concatenate([blocks[2 * pair], blocks[2 * pair + 1]], axis=1)
        piece[pair * BLK : (pair + 1) * BLK, :] = both.astype(jnp.bfloat16)
    row = lax.broadcasted_iota(jnp.int32, (TAIL, LANES), 0)
    lane = lax.broadcasted_iota(jnp.int32, (TAIL, LANES), 1)
    codes = jnp.zeros((TAIL, LANES), jnp.float32)
    for s in range(SLOTS_B):
        code = index_ref[s, 0, 0] * KW + index_ref[s, 0, 1]
        code = jnp.where(s < count_ref[0, 0], code.astype(jnp.float32), DEAD)
        codes = jnp.where((row == 0) & (lane == z * SLOTS_B + s), code, codes)
    piece[PIECE_ROWS:, :] = codes.astype(jnp.bfloat16)
    for peer in range(RING):
        out_ref[peer] = piece[...]


def stage_kernel(ring_ref, out_ref, message, sems):
    codes = jnp.zeros((TAIL, LANES), jnp.float32)
    for z in range(RING):
        message[z * PIECE_ROWS : (z + 1) * PIECE_ROWS, :] = ring_ref[z, :PIECE_ROWS, :]
        codes = codes + ring_ref[z, PIECE_ROWS:, :].astype(jnp.float32)
    message[RING * PIECE_ROWS :, :] = codes.astype(jnp.bfloat16)
    copies = [pltpu.make_async_copy(message, out_ref.at[q], sems.at[q]) for q in range(PLANE)]
    for copy in copies:
        copy.start()
    for copy in copies:
        copy.wait()


def product_kernel(
    own_half, a_ref, index_ref, count_ref, ao_ref, oindex_ref, ocount_ref, b_ref, out_ref, codes_v, codes_s, sem
):
    col = lax.axis_index("col")
    layer = lax.axis_index("layer")
    half = layer if own_half else 1 - layer
    for q in range(PLANE):
        tail = b_ref[q, RING * PIECE_ROWS :, :].astype(jnp.float32)
        codes_v[q : q + 1, :] = tail[0:1].astype(jnp.int32)
    copy = pltpu.make_async_copy(codes_v, codes_s, sem)
    copy.start()
    out_ref[...] = jnp.zeros_like(out_ref)
    copy.wait()
    lane = lax.broadcasted_iota(jnp.int32, (BLK, LANES), 1)

    for blocks, index, count, base in (
        (a_ref, index_ref, count_ref, col * INNER_A),
        (ao_ref, oindex_ref, ocount_ref, (1 - col) * INNER_A),
    ):

        def slot(i, carry, blocks=blocks, index=index, base=base):
            row = index[0, i, 0]
            inner = base + index[0, i, 1]
            piece = inner // INNER_B
            z, q = piece // PLANE, piece % PLANE
            within = inner % INNER_B
            codes = [codes_s[q, z * SLOTS_B + s] for s in range(SLOTS_B)]
            hits = [code // KW == within for code in codes]
            mine = row // (RW // 2) == half

            @pl.when(mine & (hits[0] | hits[1] | hits[2] | hits[3]))
            def _():
                start = pl.multiple_of(z * PIECE_ROWS, PIECE_ROWS)
                at = pl.multiple_of((row % (RW // 2)) * BLK, BLK)
                a = blocks[0, i]
                for pair in range(SLOTS_B // 2):

                    @pl.when(hits[2 * pair] | hits[2 * pair + 1])
                    def _(pair=pair):
                        b = b_ref[q, pl.ds(start + pair * BLK, BLK), :]
                        terms = jnp.dot(a, b, preferred_element_type=jnp.float32)
                        for side in range(2):
                            s = 2 * pair + side

                            @pl.when(hits[s])
                            def _(s=s, side=side):
                                column = codes[s] % KW
                                right = column % 2
                                moved = jnp.where(right == side, terms, pltpu.roll(terms, BLK, 1))
                                kept = jnp.where(lane // BLK == right, moved, 0.0)
                                to = pl.multiple_of((column // 2) * LANES, LANES)
                                out_ref[pl.ds(at, BLK), pl.ds(to, LANES)] += kept

            return carry

        lax.fori_loop(0, count[0, 0], slot, 0)


def product_call(own_half, *operands):
    return pl.pallas_call(
        functools.partial(product_kernel, own_half),
        out_shape=jax.ShapeDtypeStruct((HALF_ROWS, COLS), jnp.float32),
        in_specs=[VMEM, SMEM, SMEM, VMEM, SMEM, SMEM, VMEM],
        out_specs=VMEM,
        scratch_shapes=[
            pltpu.VMEM((PLANE, LANES), jnp.int32),
            pltpu.SMEM((PLANE, LANES), jnp.int32),
            pltpu.SemaphoreType.DMA,
        ],
        cost_estimate=pl.CostEstimate(flops=100_000_000, bytes_accessed=4_000_000, transcendentals=0),
        compiler_params=pltpu.CompilerParams(vmem_limit_bytes=24 * 1024 * 1024),
        name="own_half" if own_half else "other_half",
    )(*operands)


def finish_kernel(own_ref, got_ref, out_ref):
    out_ref[...] = (own_ref[...] + got_ref[...]).astype(out_ref.dtype)


def on_device(a_blocks, a_index, a_count, b_blocks, b_index, b_count):
    swap = [(0, 1), (1, 0)]
    a_other = lax.ppermute(a_blocks, "col", swap)
    index_other = lax.ppermute(a_index, "col", swap)
    count_other = lax.ppermute(a_count, "col", swap)

    to_ring = pl.pallas_call(
        pack_kernel,
        out_shape=jax.ShapeDtypeStruct((RING, PIECE_ROWS + TAIL, LANES), jnp.bfloat16),
        in_specs=[VMEM, SMEM, SMEM],
        out_specs=VMEM,
        scratch_shapes=[pltpu.VMEM((PIECE_ROWS + TAIL, LANES), jnp.bfloat16)],
        name="pack",
    )(b_blocks, b_index, b_count)
    from_ring = lax.all_to_all(to_ring, "row", 0, 0, axis_index_groups=Z_GROUPS)
    to_plane = pl.pallas_call(
        stage_kernel,
        out_shape=jax.ShapeDtypeStruct((PLANE, STAGE_ROWS, LANES), jnp.bfloat16),
        in_specs=[VMEM],
        out_specs=ANY,
        scratch_shapes=[
            pltpu.VMEM((STAGE_ROWS, LANES), jnp.bfloat16),
            pltpu.SemaphoreType.DMA((PLANE,)),
        ],
        name="stage",
    )(from_ring)
    b_all = lax.all_to_all(to_plane, "row", 0, 0, axis_index_groups=PLANE_GROUPS)

    operands = (a_blocks, a_index, a_count, a_other, index_other, count_other, b_all)
    sent = product_call(False, *operands)
    got = lax.ppermute(sent, "layer", swap)
    own = product_call(True, *operands)
    return pl.pallas_call(
        finish_kernel,
        out_shape=jax.ShapeDtypeStruct((HALF_ROWS, COLS), jnp.bfloat16),
        in_specs=[VMEM, VMEM],
        out_specs=VMEM,
        name="finish",
    )(own, got)


def solution(mesh):
    in_specs = (
        P("row", ("col", "layer"), None, None),
        P("row", ("col", "layer"), None),
        P("row", ("col", "layer")),
        P(("row", "layer"), "col", None, None),
        P(("row", "layer"), "col", None),
        P(("row", "layer"), "col"),
    )
    out_specs = P(("row", "layer"), "col")
    return jax.shard_map(
        on_device, mesh=mesh, in_specs=in_specs, out_specs=out_specs, check_vma=False
    )
```

time: 257 us -> 79.8 us (0.31)
  the two profiles are of different devices: /device:TPU:2 before, /device:TPU:12 now
where the time goes in v1:
time: 79.8 us; the launch traced here: 79.4 us
  waiting for transfers between devices  28.2 us (35%)
  blocking collectives  21.1 us (26%)
  Pallas kernels  18.3 us (23%)
  starting transfers between devices  8.17 us (10%)
  local copies, waits for them, and re-layouts  2.23 us (3%)
  between operations  1.38 us (2%)
    all_to_all x1, waiting for transfers between devices, on_device(): lax.all_to_all(to_plane, 'row', 0, 0, axis_index_groups=PLANE_GROUPS)  21.2 us
    all_to_all x1, blocking collectives, on_device(): from_ring = lax.all_to_all(to_ring, 'row', 0, 0, axis_index_groups=Z_GROUPS)  21.1 us
    pallas_call x2, Pallas kernels, product_call(): pl.pallas_call(functools.partial(product_kernel, own_half), out_shape=jax...  12.2 us
    all_to_all x1, starting transfers between devices, on_device(): lax.all_to_all(to_plane, 'row', 0, 0, axis_index_groups=PLANE_GROUPS)  7.46 us
    ppermute x1, waiting for transfers between devices, on_device(): got = lax.ppermute(sent, 'layer', swap)  6.37 us
    pallas_call x1, Pallas kernels, on_device(): pl.pallas_call(stage_kernel, out_shape=jax.ShapeDtypeStruct((PLANE, STAGE...  2.4 us
    unnamed x8, local copies, waits for them, and re-layouts  2.23 us
    pallas_call x1, Pallas kernels, on_device(): pl.pallas_call(finish_kernel, out_shape=jax.ShapeDtypeStruct((HALF_ROWS,...  1.95 us
  transfers between devices with their start and end apart: 5, of which 3 were waited for; matrix products, arithmetic and copies ran while one was open for 0% of the time, Pallas kernels for 8%

profile of v1, /device:TPU:12, one launch (start us, length us, event | category | flops | bytes accessed | tf_op | source)
XLA Modules:
  0.0 79.4 jit_solution(2219034034885407790)
XLA Ops:
  0.0 1.3 %copy.8.index_ref = s32[4,1,2]{2,1,0:T(1,128)} copy(s32[4,1,2]{0,2,1:T(2,128)} %param.10) | data formatting | bytes 64 | tf_op args[4]
  2.0 1.7 %pack.1 = bf16[8,144,128]{2,1,0:T(8,128)(2,1)} custom-call(bf16[4,1,64,64]{3,2,1,0:T(8,128)(2,1)} %b_ref.1, s32[4,1,2]{2,1,0:T(1,128)} %copy.8.index_ref, s32[1,1]{1,0:T(1,128)S(6)} %copy.12.count_ref), custom_call_target="tpu_custom_call" | custom-call | tf_op jit(solution)/shard_map/pack/pallas_call | solution.py:151
  3.7 21.1 %all_to_all.10.ring_ref = bf16[8,144,128]{2,1,0:T(8,128)(2,1)} all-to-all(bf16[8,144,128]{2,1,0:T(8,128)(2,1)} %pack.1), channel_id=1, replica_groups={{0,32,64,96,128,160,192,224},{4,36,68,100,132,164,196,228},{8,40,72,104..., dimensions={0} | all-to-all | bytes 589824 | tf_op jit(solution)/shard_map/all_to_all | solution.py:159
  24.8 2.4 %stage.1 = bf16[8,1040,128]{2,1,0:T(8,128)(2,1)} custom-call(bf16[8,144,128]{2,1,0:T(8,128)(2,1)} %all_to_all.10.ring_ref), custom_call_target="tpu_custom_call" | custom-call | tf_op jit(solution)/shard_map/stage/pallas_call | solution.py:160
  27.2 0.0 copy-start.1
  27.2 0.0 copy-start.2
  27.3 7.5 %all-to-all-start.1 = ((bf16[8,1040,128]{2,1,0:T(8,128)(2,1)}), bf16[8,1040,128]{2,1,0:T(8,128)(2,1)S(1)}, u32[]{:S(2)}, u32[]{:S(2)}) async-start(bf16[8,1040,128]{2,1,0:T(8,128)(2,1)} %stage.1), calls=%async_computation.1 | async-start | bytes 4259840 | tf_op jit(solution)/shard_map/all_to_all | solution.py:171
  34.7 0.0 copy-done.1
  34.7 0.0 collective-permute-start
  34.7 0.0 copy-done.2
  34.7 0.1 copy.9.index_ref
  34.8 0.5 collective-permute-start.1
  35.3 0.1 collective-permute-start.2
  36.1 0.6 collective-permute-done.2.ocount_ref
  36.7 0.0 collective-permute-done.1.oindex_ref
  36.7 0.0 collective-permute-done.ao_ref
  36.7 21.2 %all-to-all-done.1.b_ref = bf16[8,1040,128]{2,1,0:T(8,128)(2,1)S(1)} async-done(((bf16[8,1040,128]{2,1,0:T(8,128)(2,1)}), bf16[8,1040,128]{2,1,0:T(8,128)(2,1)S(1)}, u32[]{:S(2)}, u32[]{:S(2)}) %all-to-all-start.1) | async-done | bytes 2129952 | tf_op jit(solution)/shard_map/all_to_all | solution.py:171
  57.9 5.8 %other_half.1 = f32[256,512]{1,0:T(8,128)S(1)} custom-call(bf16[1,32,64,64]{3,2,1,0:T(8,128)(2,1)S(1)} %copy-done.1, s32[1,32,2]{2,1,0:T(8,128)S(1)} %copy.9.index_ref, s32[1,1]{1,0:T(1,128)S(6)} %copy.11.count_ref, bf16[1,32,64,64]{3,2,1,0:T(8,128)(2,1)S(1)} %collective-permute-done.ao_ref, s32[1,32,2]{2,1,0:T(8,128)S(1)} %collective-permute-done.1.oindex_ref, ...), custom_call_target="tpu_custom_call" | custom-call | flops 100000000 | bytes 4000000 | tf_op jit(solution)/shard_map/other_half/pallas_call | solution.py:125
  63.7 0.1 collective-permute-start.3
  63.8 6.5 %own_half.1.own_ref = f32[256,512]{1,0:T(8,128)S(1)} custom-call(bf16[1,32,64,64]{3,2,1,0:T(8,128)(2,1)S(1)} %copy-done.1, s32[1,32,2]{2,1,0:T(8,128)S(1)} %copy.9.index_ref, s32[1,1]{1,0:T(1,128)S(6)} %copy.11.count_ref, bf16[1,32,64,64]{3,2,1,0:T(8,128)(2,1)S(1)} %collective-permute-done.ao_ref, s32[1,32,2]{2,1,0:T(8,128)S(1)} %collective-permute-done.1.oindex_ref, ...), custom_call_target="tpu_custom_call" | custom-call | flops 100000000 | bytes 4000000 | tf_op jit(solution)/shard_map/own_half/pallas_call | solution.py:125
  70.3 0.0 copy-start
  70.3 0.8 copy-done
  71.1 6.4 %collective-permute-done.3.got_ref = f32[256,512]{1,0:T(8,128)} collective-permute-done((f32[256,512]{1,0:T(8,128)S(1)}, f32[256,512]{1,0:T(8,128)}, u32[]{:S(2)}, u32[]{:S(2)}) %collective-permute-start.3) | collective-permute-done | bytes 524320 | tf_op jit(solution)/shard_map/ppermute | solution.py:175
  77.4 1.9 %finish.1 = bf16[256,512]{1,0:T(8,128)(2,1)} custom-call(f32[256,512]{1,0:T(8,128)} %copy-done, f32[256,512]{1,0:T(8,128)} %collective-permute-done.3.got_ref), custom_call_target="tpu_custom_call" | custom-call | tf_op jit(solution)/shard_map/finish/pallas_call | solution.py:177
Async XLA Ops:
  27.2 7.5 %copy-start.1 = (bf16[1,32,64,64]{3,2,1,0:T(8,128)(2,1)S(1)}, bf16[1,32,64,64]{3,2,1,0:T(8,128)(2,1)}, u32[]{:S(2)}) copy-start(bf16[1,32,64,64]{3,2,1,0:T(8,128)(2,1)} %a_ref.3) | copy-start | bytes 786436
  27.2 7.5 %copy-start.2 = (s32[1,32,2]{1,2,0:T(2,128)S(1)}, s32[1,32,2]{1,2,0:T(2,128)}, u32[]{:S(2)}) copy-start(s32[1,32,2]{1,2,0:T(2,128)} %param.7) | copy-start | bytes 772
  27.3 30.7 %all-to-all-start.1 = ((bf16[8,1040,128]{2,1,0:T(8,128)(2,1)}), bf16[8,1040,128]{2,1,0:T(8,128)(2,1)S(1)}, u32[]{:S(2)}, u32[]{:S(2)}) async-start(bf16[8,1040,128]{2,1,0:T(8,128)(2,1)} %stage.1), calls=%async_computation.1 | async-start | bytes 4259840 | tf_op jit(solution)/shard_map/all_to_all | solution.py:171
  34.7 2.0 %collective-permute-start = (bf16[1,32,64,64]{3,2,1,0:T(8,128)(2,1)S(1)}, bf16[1,32,64,64]{3,2,1,0:T(8,128)(2,1)S(1)}, u32[]{:S(2)}, u32[]{:S(2)}) collective-permute-start(bf16[1,32,64,64]{3,2,1,0:T(8,128)(2,1)S(1)} %copy-done.1), channel_id=1, source_target_pairs={{0,2},{2,0},{1,3},{3,1},{4,6},{6,4},{5,7},{7,5},{8,10},{10,8},{9,1... | collective-permute-start | bytes 786440 | tf_op jit(solution)/shard_map/ppermute | solution.py:147
  34.8 1.9 %collective-permute-start.1 = (s32[1,32,2]{2,1,0:T(8,128)S(1)}, s32[1,32,2]{2,1,0:T(8,128)S(1)}, u32[]{:S(2)}, u32[]{:S(2)}) collective-permute-start(s32[1,32,2]{2,1,0:T(8,128)S(1)} %copy.9.index_ref), channel_id=1, source_target_pairs={{0,2},{2,0},{1,3},{3,1},{4,6},{6,4},{5,7},{7,5},{8,10},{10,8},{9,1... | collective-permute-start | bytes 776 | tf_op jit(solution)/shard_map/ppermute | solution.py:148
  35.3 1.4 %collective-permute-start.2 = (s32[1,1]{1,0:T(1,128)}, s32[1,1]{1,0:T(1,128)}, u32[]{:S(2)}, u32[]{:S(2)}) collective-permute-start(s32[1,1]{1,0:T(1,128)} %param.8), channel_id=1, source_target_pairs={{0,2},{2,0},{1,3},{3,1},{4,6},{6,4},{5,7},{7,5},{8,10},{10,8},{9,1... | collective-permute-start | bytes 20 | tf_op jit(solution)/shard_map/ppermute | solution.py:149
  63.7 13.7 %collective-permute-start.3 = (f32[256,512]{1,0:T(8,128)S(1)}, f32[256,512]{1,0:T(8,128)}, u32[]{:S(2)}, u32[]{:S(2)}) collective-permute-start(f32[256,512]{1,0:T(8,128)S(1)} %other_half.1), channel_id=1, source_target_pairs={{0,1},{1,0},{2,3},{3,2},{4,5},{5,4},{6,7},{7,6},{8,9},{9,8},{10,11... | collective-permute-start | bytes 1572872 | tf_op jit(solution)/shard_map/ppermute | solution.py:175
  70.3 0.8 %copy-start = (f32[256,512]{1,0:T(8,128)}, f32[256,512]{1,0:T(8,128)S(1)}, u32[]{:S(2)}) copy-start(f32[256,512]{1,0:T(8,128)S(1)} %own_half.1.own_ref) | copy-start | bytes 1572868
